TPU v7x, 256 devices: a whole 4x4x8 slice. The times are simulated.
256 devices in a mesh: tm: 32 (over z, x), chan: 8 (over y, core).
Axes of the slice: x: 4, y: 4, z: 8, core: 2. Of those that a mesh axis runs over, the one named last changes fastest.
Arguments:
- spectra: bfloat16 [16384, 8192], P('tm', 'chan'), may hold values from -6 to 6
- chan_weight: float32 [8192], P('chan'), may hold values from 0.25 to 4
- routes: int32 [1024, 1], P('tm'), may hold values from 0 to 31; in each aligned block of 32 rows (0 to 31, 32 to 63, ...) at most 2 rows name the same one
- offsets: int32 [16384], P('tm'), may hold values from 0 to 64
- kernel: bfloat16 [16], replicated, may hold values from 0.19921875 to 1
- gal_pix: int32 [256], replicated, may hold values from 0 to 2047
- gal_chan: int32 [256], replicated, may hold values from 64 to 8127, as said below
Outputs:
- sky_map: bfloat16 [2048, 8192], P('tm', 'chan')
- stacked: float32 [128], replicated
Inputs may be any that keep to these rules, and one draw needn't show every extreme that they name: `routes`: among the 32 blocks of one index of tm no tile is named more than 2 times; every tile is named by some block. `gal_chan`: channel of each galaxy's line centre.
All inputs are finite; a program needn't handle non-finite values.
Results may differ from a plain program's by a relative error of at most 0.012.
Values may be sent and summed in bfloat16 or wider, within the bound.
A program may use at most 64 MiB of HBM per device.

v0:
```python
import jax
import jax.numpy as jnp
from jax import lax
from jax.sharding import PartitionSpec as P

KMODES = 8
TP = 64
MARGIN = 8
SW = 64


two_pi = 6.283185307179586
highest = lax.Precision.HIGHEST


def extended_2(block, sides, width):
    for axis, dim in sides:
        count = lax.axis_size(axis)
        forward = [(i, i + 1) for i in range(count - 1)]
        backward = [(target, source) for source, target in forward]
        low = lax.ppermute(
            lax.slice_in_dim(block, block.shape[dim] - width, None, axis=dim), axis, forward
        )
        high = lax.ppermute(lax.slice_in_dim(block, 0, width, axis=dim), axis, backward)
        block = jnp.concatenate([low, block, high], axis=dim)
    return block


def basis_columns(chan_index, total):
    orders = jnp.arange(1, KMODES + 1, dtype=jnp.int32)
    phase = (chan_index[:, None] * orders[None, :] % total).astype(jnp.float32) * (two_pi / total)
    return jnp.concatenate([jnp.cos(phase), jnp.sin(phase)], axis=1)


def solve_modes(gram, proj):
    lower = jnp.linalg.cholesky(gram)
    middle = lax.linalg.triangular_solve(lower, proj, left_side=False, lower=True, transpose_a=True)
    return lax.linalg.triangular_solve(
        lower, middle, left_side=False, lower=True, transpose_a=False
    )


def band_matrix(row_offsets, kernel, width):
    columns = jnp.arange(width, dtype=jnp.int32)
    relative = columns[None, :] - row_offsets[:, None]
    taps = kernel.shape[0]
    inside = (relative >= 0) & (relative < taps)
    looked = jnp.take(kernel, jnp.clip(relative, 0, taps - 1).astype(jnp.int32))
    return jnp.where(inside, looked, jnp.zeros((), kernel.dtype))


def per_device(spectra, chan_weight, routes, offsets, kernel, gal_pix, gal_chan):
    rows_here, width = spectra.shape
    tiles = lax.axis_size("tm")
    nblocks = routes.shape[0]
    block_rows = rows_here // nblocks
    extent = TP + 2 * MARGIN
    chan_start = lax.axis_index("chan") * width
    basis = basis_columns(
        chan_start + jnp.arange(width, dtype=jnp.int32), width * lax.axis_size("chan")
    )
    values = spectra.astype(jnp.float32)
    gram_part = jnp.dot(basis.T * chan_weight[None, :], basis, precision=highest)
    proj_part = jnp.dot(values * chan_weight[None, :], basis, precision=highest)
    gram, proj = lax.psum((gram_part, proj_part), "chan")
    coef = solve_modes(gram, proj)
    cleaned = (values - jnp.dot(coef, basis.T, precision=highest)).astype(jnp.bfloat16)
    dest = routes[:, 0]
    block_ids = jnp.arange(nblocks, dtype=jnp.int32)
    blocks = cleaned.reshape(nblocks, block_rows, width)
    block_offsets = offsets.reshape(nblocks, block_rows)
    capacity = max(2, 2 * nblocks // tiles)
    earlier = (dest[:, None] == dest[None, :]) & (block_ids[None, :] < block_ids[:, None])
    rank = jnp.sum(earlier.astype(jnp.int32), axis=1)
    slot = dest * capacity + rank
    slot_ids = jnp.arange(tiles * capacity, dtype=jnp.int32)
    match = slot_ids[:, None] == slot[None, :]
    present = jnp.any(match, axis=1)
    source = jnp.sum(jnp.where(match, block_ids[None, :], 0), axis=1)
    send_rows = jnp.where(present[:, None, None], blocks[source], jnp.zeros((), jnp.bfloat16))
    send_offsets = jnp.where(present[:, None], block_offsets[source], 0)
    got_rows, got_offsets = (
        lax.all_to_all(send_rows, "tm", split_axis=0, concat_axis=0, tiled=True),
        lax.all_to_all(send_offsets, "tm", split_axis=0, concat_axis=0, tiled=True),
    )
    band = band_matrix(got_offsets.reshape(-1), kernel, extent).reshape(
        tiles, capacity * block_rows, extent
    )
    by_source = jnp.einsum(
        "srp,src->spc",
        band,
        got_rows.reshape(tiles, capacity * block_rows, width),
        preferred_element_type=jnp.float32,
    )
    extended = jnp.sum(by_source.astype(jnp.bfloat16).astype(jnp.float32), axis=0)
    margins = jnp.concatenate([extended[:MARGIN], extended[TP + MARGIN :]], axis=0)
    beside_all = extended_2(margins, (("tm", 0),), MARGIN)
    tile_sum = extended[MARGIN : MARGIN + TP]
    tile_sum = tile_sum.at[:MARGIN].add(beside_all[:MARGIN])
    tile_sum = tile_sum.at[TP - MARGIN :].add(beside_all[3 * MARGIN :])
    sky_tile = tile_sum.astype(jnp.bfloat16)
    rimmed = extended_2(sky_tile, (("chan", 1),), SW)
    local_pix = gal_pix - lax.axis_index("tm") * TP
    local_chan = gal_chan - chan_start
    owned = (local_pix >= 0) & (local_pix < TP) & (local_chan >= 0) & (local_chan < width)
    picker = (
        (jnp.arange(TP, dtype=jnp.int32)[None, :] == local_pix[:, None]) & owned[:, None]
    ).astype(jnp.bfloat16)
    picked = jnp.dot(picker, rimmed, preferred_element_type=jnp.float32)
    index = (
        jnp.clip(local_chan, 0, width - 1)[:, None] + jnp.arange(2 * SW, dtype=jnp.int32)[None, :]
    )
    windows = jnp.take_along_axis(picked, index, axis=1)
    stacked = lax.psum(jnp.sum(windows, axis=0), ("tm", "chan")) / gal_pix.shape[0]
    return (sky_tile, stacked)


def solution(mesh):
    in_specs = (P("tm", "chan"), P("chan"), P("tm", None), P("tm"), P(), P(), P())
    out_specs = (P("tm", "chan"), P())
    return jax.shard_map(
        per_device, mesh=mesh, in_specs=in_specs, out_specs=out_specs, check_vma=False
    )
```

profile of v0, /device:TPU:1, one launch (start us, length us, event | category | flops | bytes accessed | tf_op | source)
XLA Modules:
  0.0 470.9 jit_solution(15653160251686842352)
XLA Ops:
  0.6 0.0 copy-start
  0.6 0.9 convert_reduce_fusion.1
  1.6 0.7 multiply_add_fusion
  2.2 0.1 select_reduce_fusion
  2.3 0.1 fusion.81
  2.4 0.8 reshape.252
  3.2 0.1 broadcast_in_dim.73
  3.3 0.6 gather_fusion
  3.9 0.7 broadcast_select_fusion.1
  4.6 11.9 %all-to-all-start = ((s32[32,2,16]{2,1,0:T(2,128)}), s32[32,2,16]{2,1,0:T(2,128)S(1)}, u32[]{:S(2)}, u32[]{:S(2)}) async-start(s32[32,2,16]{2,1,0:T(2,128)} %broadcast_select_fusion.1), calls=%async_computation | async-start | bytes 65536 | tf_op jit(solution)/shard_map/all_to_all | solution.py:84
  16.5 0.2 fusion.80
  16.8 0.9 fusion.69
  17.6 3.3 fusion
  20.9 23.7 %all-reduce = (f32[512,16]{0,1:T(8,128)S(1)}, f32[16,16]{0,1:T(8,128)S(1)}) all-reduce(f32[512,16]{0,1:T(8,128)S(1)} %fusion, f32[16,16]{0,1:T(8,128)S(1)} %fusion.69), channel_id=1, replica_groups=mesh['tm'=32,'chan'=8] {'chan'}, use_global_device_ids=true, to_apply=%region_3.4 | all-reduce | flops 8448 | bytes 67584 | tf_op jit(solution)/shard_map/psum | solution.py:65
  44.6 0.1 copy.24
  44.7 1.5 cholesky.16
  46.1 0.6 compare_reduce_fusion
  46.8 0.6 fusion.83
  47.4 1.2 custom-call.8
  48.7 0.2 fusion.86
  48.9 0.2 fusion.84
  49.1 0.0 copy-done
  49.1 1.9 fusion.1
  51.0 0.7 gather_fusion.1
  51.7 1.6 broadcast_select_fusion
  53.2 0.0 copy-start.2
  53.2 0.0 copy-start.3
  53.2 0.0 all-to-all-done
  53.3 9.0 %all-to-all-start.1 = ((bf16[64,16,1024]{2,1,0:T(8,128)(2,1)}), bf16[64,16,1024]{2,1,0:T(8,128)(2,1)S(1)}, u32[]{:S(2)}, u32[]{:S(2)}) async-start(bf16[64,16,1024]{2,1,0:T(8,128)(2,1)} %broadcast_select_fusion), calls=%async_computation.1 | async-start | bytes 4194304 | tf_op jit(solution)/shard_map/all_to_all | solution.py:83
  62.3 0.0 copy-done.2
  62.3 0.7 fusion.100
  63.0 0.0 copy-done.3
  63.0 0.1 copy.21
  63.1 0.1 copy.22
  63.2 0.1 sub.54
  63.3 10.7 %fusion.31 = bf16[1024,80]{1,0:T(8,128)(2,1)S(1)} fusion(s32[1024]{0:T(1024)S(1)} %sub.54, bf16[]{:T(256)} %bitcast.23, bf16[]{:T(256)} %bitcast.24, bf16[]{:T(256)} %bitcast.25, bf16[]{:T(256)} %bitcast.26, bf16[]{:T(256)} %bitcast.27, bf16[]{:T(256)} %bitcast.29, bf16[]{:T(256)} %bitcast.28, bf16[]{:T(256)} %bitcast.6, bf16[]{:T(256)} %bitcast.8, ...), kind=kLoop, calls=%fused_computation.41 | loop fusion | flops 2867200 | bytes 167968 | tf_op jit(solution)/shard_map/jit(_take)/gather | solution.py:48
  74.0 33.9 %all-to-all-done.1 = bf16[64,16,1024]{2,1,0:T(8,128)(2,1)S(1)} async-done(((bf16[64,16,1024]{2,1,0:T(8,128)(2,1)}), bf16[64,16,1024]{2,1,0:T(8,128)(2,1)S(1)}, u32[]{:S(2)}, u32[]{:S(2)}) %all-to-all-start.1) | async-done | bytes 2097184 | tf_op jit(solution)/shard_map/all_to_all | solution.py:83
  107.9 0.0 copy-start.4
  107.9 2.4 convert_reduce_fusion
  110.4 6.3 %collective-permute-start = (f32[8,1024]{1,0:T(8,128)S(1)}, f32[8,1024]{1,0:T(8,128)S(1)}, u32[]{:S(2)}, u32[]{:S(2)}) collective-permute-start(f32[8,1024]{1,0:T(8,128)S(1)} %get-tuple-element.31), channel_id=1, source_target_pairs={{0,8},{8,16},{16,24},{24,32},{32,40},{40,48},{48,56},{56,64},{64,7... | collective-permute-start | bytes 98312 | tf_op jit(solution)/shard_map/ppermute | solution.py:21
  116.7 0.1 fusion.59
  116.8 1.3 collective-permute-start.1
  118.1 0.0 collective-permute-done
  118.1 3.3 collective-permute-done.1
  121.5 0.0 copy-start.1
  121.5 0.1 fusion.99
  121.6 3.8 collective-permute-start.2
  125.4 3.2 collective-permute-start.3
  128.6 0.0 copy-done.4
  128.6 0.0 collective-permute-done.2
  128.6 1.8 collective-permute-done.3
  130.4 0.2 concatenate.11
  130.6 0.4 fusion.67
  131.0 259.0 %gather_fusion.2 = f32[32768]{0:T(1024)S(1)} fusion(f32[256,1152]{1,0:T(8,128)S(1)} %fusion.67, s32[32768]{0:T(1024)S(1)} %fusion.59), kind=kCustom, calls=%fused_computation.2 | custom fusion | bytes 524288 | tf_op jit(solution)/shard_map/jit(take_along_axis)/gather | solution.py:113
  389.9 0.0 copy-done.1
  390.0 0.1 fusion.60
  390.1 80.3 %psum.23 = f32[128]{0:T(128)S(1)} all-reduce(f32[128]{0:T(128)S(1)} %fusion.60), channel_id=1, replica_groups=mesh['tm'=32,'chan'=8] {'tm','chan'}, use_global_device_ids=true, to_apply=%region_9.10 | all-reduce | flops 128 | bytes 1024 | tf_op jit(solution)/shard_map/psum | solution.py:114
  470.4 0.5 broadcast_multiply_fusion
  (13 shorter events, 0.1 us)
Async XLA Ops:
  0.6 48.5 %copy-start = (bf16[512,1024]{1,0:T(8,128)(2,1)S(1)}, bf16[512,1024]{1,0:T(8,128)(2,1)}, u32[]{:S(2)}) copy-start(bf16[512,1024]{1,0:T(8,128)(2,1)} %param.11) | copy-start | bytes 3145732
  4.6 48.6 %all-to-all-start = ((s32[32,2,16]{2,1,0:T(2,128)}), s32[32,2,16]{2,1,0:T(2,128)S(1)}, u32[]{:S(2)}, u32[]{:S(2)}) async-start(s32[32,2,16]{2,1,0:T(2,128)} %broadcast_select_fusion.1), calls=%async_computation | async-start | bytes 65536 | tf_op jit(solution)/shard_map/all_to_all | solution.py:84
  53.2 9.1 %copy-start.2 = (bf16[16]{0:T(256)(128)(2,1)S(1)}, bf16[16]{0:T(256)(128)(2,1)}, u32[]{:S(2)}) copy-start(bf16[16]{0:T(256)(128)(2,1)} %param.15) | copy-start | bytes 100
  53.2 9.8 %copy-start.3 = (s32[256]{0:T(256)S(1)}, s32[256]{0:T(256)}, u32[]{:S(2)}) copy-start(s32[256]{0:T(256)} %param.17) | copy-start | bytes 3076
  53.3 54.7 %all-to-all-start.1 = ((bf16[64,16,1024]{2,1,0:T(8,128)(2,1)}), bf16[64,16,1024]{2,1,0:T(8,128)(2,1)S(1)}, u32[]{:S(2)}, u32[]{:S(2)}) async-start(bf16[64,16,1024]{2,1,0:T(8,128)(2,1)} %broadcast_select_fusion), calls=%async_computation.1 | async-start | bytes 4194304 | tf_op jit(solution)/shard_map/all_to_all | solution.py:83
  107.9 20.6 %copy-start.4 = (s32[256]{0:T(256)S(1)}, s32[256]{0:T(256)}, u32[]{:S(2)}) copy-start(s32[256]{0:T(256)} %param.16) | copy-start | bytes 3076
  110.4 7.7 %collective-permute-start = (f32[8,1024]{1,0:T(8,128)S(1)}, f32[8,1024]{1,0:T(8,128)S(1)}, u32[]{:S(2)}, u32[]{:S(2)}) collective-permute-start(f32[8,1024]{1,0:T(8,128)S(1)} %get-tuple-element.31), channel_id=1, source_target_pairs={{0,8},{8,16},{16,24},{24,32},{32,40},{40,48},{48,56},{56,64},{64,7... | collective-permute-start | bytes 98312 | tf_op jit(solution)/shard_map/ppermute | solution.py:21
  116.8 4.7 collective-permute-start.1
  121.5 268.4 %copy-start.1 = (bf16[64,1024]{1,0:T(8,128)(2,1)}, bf16[64,1024]{1,0:T(8,128)(2,1)S(1)}, u32[]{:S(2)}) copy-start(bf16[64,1024]{1,0:T(8,128)(2,1)S(1)} %convert_element_type.28) | copy-start | bytes 393220
  121.6 7.0 %collective-permute-start.2 = (bf16[64,64]{1,0:T(8,128)(2,1)S(1)}, bf16[64,64]{1,0:T(8,128)(2,1)S(1)}, u32[]{:S(2)}, u32[]{:S(2)}) collective-permute-start(bf16[64,64]{1,0:T(8,128)(2,1)S(1)} %get-tuple-element.33), channel_id=1, source_target_pairs={{0,1},{1,2},{2,3},{3,4},{4,5},{5,6},{6,7},{8,9},{9,10},{10,11},{11... | collective-permute-start | bytes 24584 | tf_op jit(solution)/shard_map/ppermute | solution.py:21
  125.4 5.1 %collective-permute-start.3 = (bf16[64,64]{1,0:T(8,128)(2,1)S(1)}, bf16[64,64]{1,0:T(8,128)(2,1)S(1)}, u32[]{:S(2)}, u32[]{:S(2)}) collective-permute-start(bf16[64,64]{1,0:T(8,128)(2,1)S(1)} %get-tuple-element.32), channel_id=1, source_target_pairs={{1,0},{2,1},{3,2},{4,3},{5,4},{6,5},{7,6},{9,8},{10,9},{11,10},{12... | collective-permute-start | bytes 24584 | tf_op jit(solution)/shard_map/ppermute | solution.py:24
where the time goes:
time: 472 us; the launch traced here: 471 us
  local copies, waits for them, and re-layouts  262 us (56%)
  blocking collectives  104 us (22%)
  waiting for transfers between devices  39.1 us (8%)
  starting transfers between devices  35.4 us (8%)
  other arithmetic  19.8 us (4%)
  matrix products  9.19 us (2%)
    gather x1, local copies, waits for them, and re-layouts, per_device(): windows = jnp.take_along_axis(picked, index, axis=1)  259 us
    psum x1, blocking collectives, per_device(): lax.psum(jnp.sum(windows, axis=0), ('tm', 'chan')) / gal_pix.shape[0]  80.3 us
    all_to_all x1, waiting for transfers between devices, per_device(): lax.all_to_all(send_rows, 'tm', split_axis=0, concat_axis=0, tiled=True)  33.9 us
    psum x1, blocking collectives, per_device(): gram, proj = lax.psum((gram_part, proj_part), 'chan')  23.7 us
    all_to_all x1, starting transfers between devices, per_device(): lax.all_to_all(send_offsets, 'tm', split_axis=0, concat_axis=0, tiled=True)  11.9 us
    gather x1, other arithmetic, band_matrix(): looked = jnp.take(kernel, jnp.clip(relative, 0, taps - 1).astype(jnp.int32))  10.7 us
    ppermute x2, starting transfers between devices, extended_2(): lax.ppermute(lax.slice_in_dim(block, block.shape[dim] - width, None, axis...  10.1 us
  transfers between devices with their start and end apart: 6, of which 3 were waited for; matrix products, arithmetic and copies ran while one was open for 5% of the time, Pallas kernels for 0%

commit v1 on v0

v1 whole, which is shorter than its diff:
```python
import jax
import jax.numpy as jnp
from jax import lax
from jax.experimental import pallas as pl
from jax.experimental.pallas import tpu as pltpu
from jax.sharding import PartitionSpec as P

KMODES = 8
MODES = 2 * KMODES
TP = 64
MARGIN = 8
SW = 64
TAPS = 16
NX = 4

two_pi = 6.283185307179586
highest = lax.Precision.HIGHEST
MESH = pl.DeviceIdType.MESH
f32 = jnp.float32
bf16 = jnp.bfloat16


def basis_rows(chan_index, total):
    orders = jnp.arange(1, KMODES + 1, dtype=jnp.int32)
    phase = (orders[:, None] * chan_index[None, :] % total).astype(f32) * (two_pi / total)
    return jnp.concatenate([jnp.cos(phase), jnp.sin(phase)], axis=0)


def split3(value):
    high = value.astype(bf16)
    rest = value - high.astype(f32)
    mid = rest.astype(bf16)
    low = (rest - mid.astype(f32)).astype(bf16)
    return high, mid, low


def iota(shape, dim):
    return lax.broadcasted_iota(jnp.int32, shape, dim)


def make_kernel(tm_size, chan_size, rows, width, nblocks, ngal):
    nz = tm_size // NX
    quarter = width // NX
    npix = tm_size * TP
    zpix = NX * TP
    half = zpix // 2
    block_rows = rows // nblocks
    shifts = quarter + 2 * SW

    def kernel(
        spec, weight, routes, offsets, taps, gal_pix, gal_chan, basis,
        sky, stacked,
        own, pix, raw, gram, proj, ext, coef, band, clean, part, counts,
        zsend, zrecv, final, st1, st2, st3,
        own_sem, pix_s, pix_r, raw_s, raw_r, gram_s, gram_r, proj_s, proj_r, coef_s, coef_r,
        z_s, z_r, fin_s, fin_r, st1_s, st1_r, st2_s, st2_r, st3_s, st3_r,
    ):
        tm = lax.axis_index("tm")
        j = lax.axis_index("chan")
        z = lax.div(tm, NX)
        x = lax.rem(tm, NX)

        def x_peer(r):
            return (z * NX + lax.rem(x + r, NX), j)

        def c_peer(r):
            return (tm, lax.rem(j + r, chan_size))

        def z_peer(r):
            return (lax.rem(z + r, nz) * NX + x, j)

        peers = (
            [x_peer(r) for r in range(1, NX)]
            + [c_peer(r) for r in range(1, chan_size)]
            + [z_peer(r) for r in range(1, nz)]
        )
        barrier = pltpu.get_barrier_semaphore()
        for peer in peers:
            pl.semaphore_signal(barrier, inc=1, device_id=peer, device_id_type=MESH)

        def remote(src, dst, send_sem, recv_sem, peer):
            return pltpu.make_async_remote_copy(
                src_ref=src, dst_ref=dst, send_sem=send_sem, recv_sem=recv_sem,
                device_id=peer, device_id_type=MESH,
            )

        load = pltpu.make_async_copy(spec, own, own_sem)
        load.start()

        inside = iota((nblocks, rows), 1) - block_rows * iota((nblocks, rows), 0)
        owner = (inside >= 0) & (inside < block_rows)
        tile = jnp.sum(jnp.where(owner, routes[...], 0), axis=0, keepdims=True)
        pix[0] = tile * TP + offsets[...] - MARGIN

        weighted = basis[...] * weight[...]
        gram[0] = jnp.zeros((MODES, 128), f32)
        gram[0, :, 0:MODES] = lax.dot_general(
            weighted, basis[...], (((1,), (1,)), ((), ())), precision=highest,
            preferred_element_type=f32,
        )
        w_stack = jnp.concatenate(split3(weighted), axis=0)
        ext[...] = jnp.zeros(ext.shape, f32)

        pl.semaphore_wait(barrier, len(peers))

        sends = []

        def start(copy):
            copy.start()
            sends.append(copy)

        for r in range(1, NX):
            start(remote(pix.at[0], pix.at[NX - r], pix_s.at[r], pix_r.at[NX - r], x_peer(r)))
        for r in (2, 1, 3):
            column = pl.multiple_of(lax.rem(x + r, NX) * quarter, quarter)
            start(remote(
                spec.at[:, pl.ds(column, quarter)], raw.at[NX - r], raw_s.at[r], raw_r.at[NX - r],
                x_peer(r),
            ))
        for r in range(1, chan_size):
            start(remote(
                gram.at[0], gram.at[chan_size - r], gram_s.at[r], gram_r.at[chan_size - r],
                c_peer(r),
            ))

        load.wait()
        products = lax.dot_general(
            w_stack, own[...], (((1,), (1,)), ((), ())), preferred_element_type=f32
        )
        proj[0] = products[:MODES] + products[MODES:2 * MODES] + products[2 * MODES:]
        for r in range(1, chan_size):
            start(remote(
                proj.at[0], proj.at[chan_size - r], proj_s.at[r], proj_r.at[chan_size - r],
                c_peer(r),
            ))

        def build_band(slot):
            first = pix[slot]
            group = jnp.broadcast_to(first >> 4, (TAPS, rows))
            inner = jnp.broadcast_to(first & (TAPS - 1), (TAPS, rows))
            lane = iota((TAPS, rows), 0)
            turn = (lane - inner) & (TAPS - 1)
            tap = jnp.zeros((TAPS, rows), f32)
            values = taps[...].astype(f32)
            for m in range(TAPS):
                tap = jnp.where(turn == m, values[0:1, m:m + 1], tap)
            where = jnp.where(lane < inner, group + 1, group)

            def step(a, carry):
                row = pl.multiple_of(a * TAPS, TAPS)
                band[pl.ds(row, TAPS), slot * rows:(slot + 1) * rows] = jnp.where(
                    where == a, tap, 0.0
                ).astype(bf16)
                return carry

            lax.fori_loop(0, npix // TAPS, step, 0, unroll=4)

        build_band(0)

        for r in range(1, chan_size):
            remote(gram.at[0], gram.at[r], gram_s.at[r], gram_r.at[r], c_peer(r)).wait_recv()
        total = gram[0]
        for r in range(1, chan_size):
            total = total + gram[r]
        row_id = iota((MODES, 128), 0)
        both = jnp.where(iota((MODES, 128), 1) - MODES == row_id, 1.0, total)
        for i in range(MODES):
            pivot = both[i:i + 1, :] / both[i:i + 1, i:i + 1]
            both = jnp.where(row_id == i, pivot, both - both[:, i:i + 1] * pivot)

        for r in range(1, chan_size):
            remote(proj.at[0], proj.at[r], proj_s.at[r], proj_r.at[r], c_peer(r)).wait_recv()
        full = proj[0]
        for r in range(1, chan_size):
            full = full + proj[r]
        ext[MODES:2 * MODES, :] = full
        coef[0] = jnp.dot(both, ext[...], precision=highest, preferred_element_type=f32)
        for r in range(1, NX):
            start(remote(coef.at[0], coef.at[NX - r], coef_s.at[r], coef_r.at[NX - r], x_peer(r)))

        for r in range(1, NX):
            remote(pix.at[0], pix.at[r], pix_s.at[r], pix_r.at[r], x_peer(r)).wait_recv()
            build_band(r)

        begin = gal_chan[...] - SW - (j * width + x * quarter)
        shift_hot = (iota((shifts, ngal), 0) == quarter - 1 - begin).astype(f32).astype(bf16)
        pixel_hot = (iota((npix, ngal), 0) == gal_pix[...]).astype(f32).astype(bf16)
        counts[...] = lax.dot_general(
            shift_hot, pixel_hot, (((1,), (1,)), ((), ())), preferred_element_type=f32
        ).astype(bf16)

        here = pl.multiple_of(x * quarter, quarter)
        b_high, b_mid, b_low = split3(basis[:, pl.ds(here, quarter)])
        b_stack = jnp.concatenate(
            [b_high, b_mid, b_high, b_mid, b_low, b_high, jnp.zeros((2 * MODES, quarter), bf16)],
            axis=0,
        )

        def clean_slot(slot, values):
            c_high, c_mid, c_low = split3(coef[slot])
            c_stack = jnp.concatenate(
                [c_high, c_high, c_mid, c_mid, c_high, c_low, jnp.zeros((2 * MODES, rows), bf16)],
                axis=0,
            )
            ripple = lax.dot_general(
                c_stack, b_stack, (((0,), (0,)), ((), ())), preferred_element_type=f32
            )
            clean[slot * rows:(slot + 1) * rows, :] = (values.astype(f32) - ripple).astype(bf16)

        clean_slot(0, own[:, pl.ds(here, quarter)])
        for r in (1, 3, 2):
            remote(coef.at[0], coef.at[r], coef_s.at[r], coef_r.at[r], x_peer(r)).wait_recv()
            remote(
                spec.at[:, pl.ds(0, quarter)], raw.at[r], raw_s.at[r], raw_r.at[r], x_peer(r)
            ).wait_recv()
            clean_slot(r, raw[r])

        def chunk_row(step):
            return pl.multiple_of(lax.rem(z + step + 2 * nz, nz) * zpix, zpix)

        def grid_chunk(step):
            row = chunk_row(step)
            part[pl.ds(row, zpix), :] = jnp.dot(
                band[pl.ds(row, zpix), :], clean[...], preferred_element_type=f32
            )

        def part_half(step, which):
            row = pl.multiple_of(chunk_row(step) + which * half, half)
            return part[pl.ds(row, half), :]

        far = nz // 2

        def z_copy(way, index):
            return remote(
                zsend.at[way, index], zrecv.at[way, index], z_s.at[way, index],
                z_r.at[way, index], z_peer((1, nz - 1)[way]),
            )

        def z_start(way, index, value):
            zsend[way, index] = value.astype(bf16)
            start(z_copy(way, index))

        def z_take(way, index):
            z_copy(way, index).wait_recv()
            return zrecv[way, index].astype(f32)

        sign = (1, -1)
        grid_chunk(far)
        for way in range(2):
            z_start(way, 0, part_half(far, way))
        for way in range(2):
            grid_chunk(sign[way] * (far - 1))
            z_start(way, far, part_half(sign[way] * (far - 1), 1 - way))

        def grid_rest(i, carry):
            grid_chunk(i + (2 - far))
            return carry

        lax.fori_loop(0, nz - 3, grid_rest, 0)

        picked = jnp.dot(counts[...], part[...].astype(bf16), preferred_element_type=f32)
        wide = jnp.concatenate([picked, jnp.zeros((shifts, 512 - quarter), f32)], axis=1)
        folded = jnp.zeros((8, 512), f32)
        for i in range(shifts // 8):
            folded = folded + pltpu.roll(
                wide[8 * i:8 * i + 8], (513 - quarter + 8 * i) % 512, 1
            )
        window = jnp.zeros((1, 512), f32)
        for i in range(8):
            window = window + (pltpu.roll(folded[i:i + 1], i, 1) if i else folded[i:i + 1])
        st1[x] = window[:, :2 * SW]

        def share(buffer, me, send_sem, recv_sem, peer_of, count):
            for r in range(1, count):
                start(remote(buffer.at[me], buffer.at[me], send_sem.at[r], recv_sem.at[me], peer_of(r)))

        def gather(buffer, me, send_sem, recv_sem, peer_of, count):
            for r in range(1, count):
                other = lax.rem(me + r, count)
                remote(
                    buffer.at[other], buffer.at[other], send_sem.at[r], recv_sem.at[other], peer_of(r)
                ).wait_recv()
            value = buffer[0]
            for i in range(1, count):
                value = value + buffer[i]
            return value

        share(st1, x, st1_s, st1_r, x_peer, NX)

        def long_step(k):
            for way in range(2):
                got = z_take(way, k)
                z_start(way, k + 1, got + part_half(sign[way] * (far - 1 - k), way))

        def short_step(k):
            for way in range(2):
                got = z_take(way, far + k)
                z_start(way, far + k + 1, got + part_half(sign[way] * (far - 2 - k), 1 - way))

        long_step(0)
        st2[j] = gather(st1, x, st1_s, st1_r, x_peer, NX)
        share(st2, j, st2_s, st2_r, c_peer, chan_size)
        short_step(0)
        long_step(1)
        st3[z] = gather(st2, j, st2_s, st2_r, c_peer, chan_size)
        share(st3, z, st3_s, st3_r, z_peer, nz)
        short_step(1)
        long_step(2)
        stacked[...] = gather(st3, z, st3_s, st3_r, z_peer, nz) / ngal

        got = [z_take(way, 2 * far - 2) for way in range(2)]
        for way in range(2):
            value = z_take(way, far - 1) + got[1 - way] + part_half(0, way)
            final[way * half:(way + 1) * half, :] = value.astype(bf16)

        place = sky.at[:, pl.ds(here, quarter)]
        for r in (2, 1, 3):
            row = pl.multiple_of(lax.rem(x + r, NX) * TP, TP)
            start(remote(
                final.at[pl.ds(row, TP), :], place, fin_s.at[r], fin_r.at[NX - r], x_peer(r)
            ))
        sky[:, pl.ds(here, quarter)] = final[pl.ds(pl.multiple_of(x * TP, TP), TP), :]
        for r in range(1, NX):
            column = pl.multiple_of(lax.rem(x + r, NX) * quarter, quarter)
            remote(
                final.at[pl.ds(0, TP), :], sky.at[:, pl.ds(column, quarter)], fin_s.at[r],
                fin_r.at[r], x_peer(r),
            ).wait_recv()
        for copy in sends:
            copy.wait_send()

    dma = pltpu.SemaphoreType.DMA
    scratch = [
        pltpu.VMEM((rows, width), bf16),
        pltpu.VMEM((NX, 1, rows), jnp.int32),
        pltpu.VMEM((NX, rows, quarter), bf16),
        pltpu.VMEM((chan_size, MODES, 128), f32),
        pltpu.VMEM((chan_size, MODES, rows), f32),
        pltpu.VMEM((128, rows), f32),
        pltpu.VMEM((NX, MODES, rows), f32),
        pltpu.VMEM((npix, NX * rows), bf16),
        pltpu.VMEM((NX * rows, quarter), bf16),
        pltpu.VMEM((npix, quarter), f32),
        pltpu.VMEM((shifts, npix), bf16),
        pltpu.VMEM((2, nz - 1, half, quarter), bf16),
        pltpu.VMEM((2, nz - 1, half, quarter), bf16),
        pltpu.VMEM((zpix, quarter), bf16),
        pltpu.VMEM((NX, 1, 2 * SW), f32),
        pltpu.VMEM((chan_size, 1, 2 * SW), f32),
        pltpu.VMEM((nz, 1, 2 * SW), f32),
        dma,
    ]
    for count in (NX, NX, chan_size, chan_size, NX):
        scratch += [dma((count,)), dma((count,))]
    scratch += [dma((2, nz - 1)), dma((2, nz - 1))]
    for count in (NX, NX, chan_size, nz):
        scratch += [dma((count,)), dma((count,))]
    return kernel, scratch


def solution(mesh):
    tm_size, chan_size = mesh.shape["tm"], mesh.shape["chan"]

    def per_device(spectra, chan_weight, routes, offsets, taps, gal_pix, gal_chan):
        rows, width = spectra.shape
        chan_start = lax.axis_index("chan") * width
        basis = basis_rows(
            chan_start + jnp.arange(width, dtype=jnp.int32), width * chan_size
        )
        kernel, scratch = make_kernel(
            tm_size, chan_size, rows, width, routes.shape[0], gal_pix.shape[0]
        )
        vmem = pl.BlockSpec(memory_space=pltpu.VMEM)
        sky, stacked = pl.pallas_call(
            kernel,
            out_shape=(
                jax.ShapeDtypeStruct((TP, width), bf16),
                jax.ShapeDtypeStruct((1, 2 * SW), f32),
            ),
            in_specs=[pl.BlockSpec(memory_space=pl.ANY)] + [vmem] * 7,
            out_specs=(vmem, vmem),
            scratch_shapes=scratch,
            compiler_params=pltpu.CompilerParams(
                collective_id=0, has_side_effects=True, vmem_limit_bytes=48 * 1024 * 1024
            ),
        )(
            spectra, chan_weight[None, :], routes, offsets[None, :], taps[None, :],
            gal_pix[None, :], gal_chan[None, :], basis,
        )
        return sky, stacked[0]

    in_specs = (
        P("tm", "chan"), P("chan"), P("tm", None), P("tm"), P(None), P(None), P(None)
    )
    return jax.shard_map(
        per_device, mesh=mesh, in_specs=in_specs, out_specs=(P("tm", "chan"), P(None)),
        check_vma=False,
    )
```

time: 472 us -> 50.5 us (0.11)
  local copies, waits for them, and re-layouts: 262 us -> 3.79 us
  blocking collectives: 104 us -> 0 us
  Pallas kernels: 0 us -> 45.6 us
  waiting for transfers between devices: 39.1 us -> 0 us
  starting transfers between devices: 35.4 us -> 0 us
  other arithmetic: 19.8 us -> 0.23 us
  matrix products: 9.19 us -> 0 us
    gather x4 -> x0, local copies, waits for them, and re-layouts: 261 us -> none  [the longest x1 259 us: per_device(): windows = jnp.take_along_axis(picked, index, axis=1)]
    psum x2 -> x0, blocking collectives: 104 us -> none  [the longest x1 80.3 us: per_device(): lax.psum(jnp.sum(windows, axis=0), ('tm', 'chan')) / gal_pix.shape[0]]
    pallas_call x0 -> x1, Pallas kernels: none -> 45.6 us  [per_device(): pl.pallas_call(kernel, out_shape=(jax.ShapeDtypeStruct((TP, width), bf16)...]
    all_to_all x2 -> x0, waiting for transfers between devices: 33.9 us -> none  [the longest x1 33.9 us: per_device(): lax.all_to_all(send_rows, 'tm', split_axis=0, concat_axis=0, tiled=True)]
    all_to_all x2 -> x0, starting transfers between devices: 20.9 us -> none  [the longest x1 11.9 us: per_device(): lax.all_to_all(send_offsets, 'tm', split_axis=0, concat_axis=0, tiled=True)]
    ppermute x4 -> x0, starting transfers between devices: 14.5 us -> none  [the longest x2 10.1 us: extended_2(): lax.ppermute(lax.slice_in_dim(block, block.shape[dim] - width, None, axis...]
    gather x3 -> x0, other arithmetic: 10.8 us -> none  [the longest x1 10.7 us: band_matrix(): looked = jnp.take(kernel, jnp.clip(relative, 0, taps - 1).astype(jnp.int32))]
    dot_general x5 -> x0, matrix products: 8.79 us -> none  [the longest x1 3.25 us: per_device(): proj_part = jnp.dot(values * chan_weight[None, :], basis, precision=highest)]
  transfers between devices with their start and end apart: 6 -> 0, of which waited for: 3 -> 0; matrix products, arithmetic and copies ran while one was open for 5% -> 0% of each run, Pallas kernels for 0% -> 0%
where the time goes in v1:
time: 50.5 us; the launch traced here: 50.4 us
  Pallas kernels  45.6 us (90%)
  local copies, waits for them, and re-layouts  3.79 us (8%)
  between operations  0.72 us (1%)
    pallas_call x1, Pallas kernels, per_device(): pl.pallas_call(kernel, out_shape=(jax.ShapeDtypeStruct((TP, width), bf16)...  45.6 us
    unnamed x17, local copies, waits for them, and re-layouts  3.79 us

profile of v1, /device:TPU:1, one launch (start us, length us, event | category | flops | bytes accessed | tf_op | source)
XLA Modules:
  0.0 50.4 jit_solution(4778449465143523091)
XLA Ops:
  0.6 0.0 copy-start.6
  0.7 0.6 %copy-done.6 = s32[32,1]{0,1:T(1,128)S(1)} copy-done((s32[32,1]{0,1:T(1,128)S(1)}, s32[32,1]{0,1:T(1,128)}, u32[]{:S(2)}) %copy-start.6) | copy-done | bytes 152
  1.3 0.1 copy.9.routes
  1.4 0.2 fusion.4
  1.6 0.0 copy-start.1
  1.6 0.0 copy-start.2
  1.6 0.0 copy-start.3
  1.6 0.0 copy-start.4
  1.7 0.0 copy-start.5
  1.7 0.6 %copy-done.1 = f32[1024]{0:T(1024)S(1)} copy-done((f32[1024]{0:T(1024)S(1)}, f32[1024]{0:T(1024)}, u32[]{:S(2)}) %copy-start.1) | copy-done | bytes 4120
  2.3 0.0 copy-done.2
  2.3 0.0 copy-done.3
  2.3 0.0 copy-done.4
  2.3 0.0 copy-done.5
  2.3 0.0 copy-start
  2.3 1.2 %copy-done = bf16[512,1024]{1,0:T(8,128)(2,1)S(1)} copy-done((bf16[512,1024]{1,0:T(8,128)(2,1)S(1)}, bf16[512,1024]{1,0:T(8,128)(2,1)}, u32[]{:S(2)}) %copy-start) | copy-done | bytes 1048600
  3.6 45.6 %shard_map.86 = (bf16[64,1024]{1,0:T(8,128)(2,1)S(1)}, f32[1,128]{1,0:T(1,128)S(1)}) custom-call(bf16[512,1024]{1,0:T(8,128)(2,1)S(1)} %copy-done, f32[1,1024]{1,0:T(1,128)S(1)} %bitcast.6, s32[32,1]{1,0:T(8,128)S(1)} %copy.9.routes, s32[1,512]{1,0:T(1,128)S(1)} %bitcast.7, bf16[1,16]{1,0:T(2,128)(2,1)S(1)} %bitcast.10, s32[1,256]{1,0:T(1,128)S(1)} %bitcast.8, ...), custom_call_target="tpu_custom_call" | custom-call | tf_op jit(solution)/shard_map/pallas_call | solution.py:374
  49.2 0.7 %copy.12 = bf16[64,1024]{1,0:T(8,128)(2,1)} copy(bf16[64,1024]{1,0:T(8,128)(2,1)S(1)} %get-tuple-element.10) | data formatting | bytes 262144
  49.9 0.5 %copy.13 = f32[128]{0:T(128)} copy(f32[128]{0:T(128)S(1)} %bitcast.11) | data formatting | bytes 1024
  (3 shorter events, 0.0 us)
Async XLA Ops:
  0.6 0.7 %copy-start.6 = (s32[32,1]{0,1:T(1,128)S(1)}, s32[32,1]{0,1:T(1,128)}, u32[]{:S(2)}) copy-start(s32[32,1]{0,1:T(1,128)} %param.9) | copy-start | bytes 388
  1.6 0.7 %copy-start.1 = (f32[1024]{0:T(1024)S(1)}, f32[1024]{0:T(1024)}, u32[]{:S(2)}) copy-start(f32[1024]{0:T(1024)} %param.8) | copy-start | bytes 12292
  1.6 0.7 %copy-start.2 = (s32[512]{0:T(512)S(1)}, s32[512]{0:T(512)}, u32[]{:S(2)}) copy-start(s32[512]{0:T(512)} %param.10) | copy-start | bytes 6148
  1.6 0.7 %copy-start.3 = (s32[256]{0:T(256)S(1)}, s32[256]{0:T(256)}, u32[]{:S(2)}) copy-start(s32[256]{0:T(256)} %param.12) | copy-start | bytes 3076
  1.6 0.7 %copy-start.4 = (s32[256]{0:T(256)S(1)}, s32[256]{0:T(256)}, u32[]{:S(2)}) copy-start(s32[256]{0:T(256)} %param.13) | copy-start | bytes 3076
  1.7 0.7 %copy-start.5 = (bf16[16]{0:T(256)(128)(2,1)S(1)}, bf16[16]{0:T(256)(128)(2,1)}, u32[]{:S(2)}) copy-start(bf16[16]{0:T(256)(128)(2,1)} %param.11) | copy-start | bytes 100
  2.3 1.2 %copy-start = (bf16[512,1024]{1,0:T(8,128)(2,1)S(1)}, bf16[512,1024]{1,0:T(8,128)(2,1)}, u32[]{:S(2)}) copy-start(bf16[512,1024]{1,0:T(8,128)(2,1)} %spec.1) | copy-start | bytes 3145732
